TPU v7x, 128 devices: a whole 4x4x4 slice. The times are simulated.
128 devices in a mesh: rep: 32 (over x, z, core), head: 4 (over y).
Axes of the slice: x: 4, y: 4, z: 4, core: 2. Of those that a mesh axis runs over, the one named last changes fastest.
Arguments:
- query: bfloat16 [288, 64, 192], P('rep', 'head'), may hold values from -3 to 3
- latent_cache: bfloat16 [256, 512, 576], P('rep'), may hold values from -51 to 51
- moved_rows: bfloat16 [32, 3072, 576], P(None, ('rep', 'head')), may hold values from -51 to 51
- target_group: int32 [32], replicated, may hold values from 0 to 31, each once
- moved_length: int32 [32], replicated, may hold values from 2 to 3072, as said below
- key_absorb: bfloat16 [64, 128, 512], P('head'), may hold values from -0.5 to 0.5
- value_head_projection: bfloat16 [64, 512, 128], P('head'), may hold values from -0.25 to 0.25
- out_proj: bfloat16 [8192, 3584], P(None, ('rep', 'head')), may hold values from -1.5 to 1.5
- residual: bfloat16 [288, 3584], P(None, ('rep', 'head')), may hold values from -16 to 16
- norm_gain: bfloat16 [3584], P(('rep', 'head')), may hold values from 0.099609375 to 1.8984375
- centroid: bfloat16 [128, 3584], P(None, ('rep', 'head')), may hold values from -0.09375 to 0.09375
- expert_ids: int32 [288, 8], replicated, may hold values from 0 to 127, all different within a row; in each aligned block of 288 rows (0 to 287, 288 to 575, ...) at most 36 rows name the same one
- up_weight: bfloat16 [128, 3584, 1024], P(('rep', 'head')), may hold values from -0.09375 to 0.09375
- down_weight: bfloat16 [128, 1024, 3584], P(('rep', 'head')), may hold values from -0.1875 to 0.1875
Outputs:
- layer_out: bfloat16 [288, 3584], P(None, ('rep', 'head'))
Inputs may be any that keep to these rules, and one draw needn't show every extreme that they name: `expert_ids`: each token names 8 different experts; over all tokens no expert is named by more than 36 rows, a bound that some block reaches. `target_group`: A permutation: every group receives exactly one migrated request. `moved_length`: some request has all 3072 rows valid.
All inputs are finite; a program needn't handle non-finite values.
Results may differ from a plain program's by a relative error of at most 0.0065.
Values may be sent and summed in bfloat16 or wider, within the bound.
A program may use at most 128 MiB of HBM per device.

v0:
```python
import math

import jax
import jax.numpy as jnp
from jax import lax
from jax.sharding import PartitionSpec as P

NOPE = 128
KV = 512
D = 3584
RES = 8


def normalize(scores):
    highest = jnp.max(scores, axis=-1, keepdims=True)
    routing_weights = jnp.exp(scores - highest)
    return (routing_weights / jnp.sum(routing_weights, axis=-1, keepdims=True)).astype(jnp.bfloat16)


def expert_slots(expert_ids, experts):
    pair_expert = expert_ids.reshape(-1)
    matches = (pair_expert[:, None] == jnp.arange(experts, dtype=jnp.int32)[None, :]).astype(
        jnp.int32
    )
    running = jnp.cumsum(matches, axis=0) - 1
    pair_slot = jnp.sum(running * matches, axis=1)
    return (pair_expert, pair_slot)


def whole_far(far_query, arrived, length, scaling_factor):
    far_scores = (
        jnp.einsum("hk,pk->hp", far_query, arrived, preferred_element_type=jnp.float32)
        * scaling_factor
    )
    usable = jnp.arange(arrived.shape[0], dtype=jnp.int32) < length
    far_scores = jnp.where(usable[None, :], far_scores, -1e30)
    return jnp.dot(
        normalize(far_scores), arrived[:, :KV], preferred_element_type=jnp.float32
    ).astype(jnp.bfloat16)


def per_device(
    query,
    latent_cache,
    moved_rows,
    target_group,
    moved_length,
    key_absorb,
    value_head_projection,
    out_proj,
    residual,
    norm_gain,
    centroid,
    expert_ids,
    up_weight,
    down_weight,
):
    rep_count = lax.axis_size("rep")
    head_count = lax.axis_size("head")
    scaling_factor = 1.0 / math.sqrt(query.shape[-1])
    group_count = target_group.shape[0]
    source = (
        jnp.zeros((group_count,), jnp.int32)
        .at[target_group]
        .set(jnp.arange(group_count, dtype=jnp.int32))
    )
    outgoing = jnp.take(moved_rows, source, axis=0)
    my_group = lax.axis_index("rep")
    length = jnp.take(moved_length, jnp.take(source, my_group))
    absorbed = jnp.einsum(
        "thn,hnk->thk", query[:, :, :NOPE], key_absorb, preferred_element_type=jnp.float32
    ).astype(jnp.bfloat16)
    joined = jnp.concatenate([absorbed, query[:, :, NOPE:]], axis=2)
    copies = jnp.broadcast_to(outgoing[:, None], (group_count, head_count) + outgoing.shape[1:])
    copies = copies.reshape((group_count * head_count,) + outgoing.shape[1:])
    landed = lax.all_to_all(copies, ("rep", "head"), split_axis=0, concat_axis=0, tiled=True)
    latent_far = whole_far(
        joined[RES], landed.reshape(-1, landed.shape[-1]), length, scaling_factor
    )
    near_scores = (
        jnp.einsum("ihk,ipk->ihp", joined[:RES], latent_cache, preferred_element_type=jnp.float32)
        * scaling_factor
    )
    latent_near = jnp.einsum(
        "ihp,ipk->ihk",
        normalize(near_scores),
        latent_cache[:, :, :KV],
        preferred_element_type=jnp.float32,
    ).astype(jnp.bfloat16)
    latent_vectors = jnp.concatenate([latent_near, latent_far[None]], axis=0)
    head_out = jnp.einsum(
        "ygf,gfw->ygw", latent_vectors, value_head_projection, preferred_element_type=jnp.float32
    ).astype(jnp.bfloat16)
    batch_rows = head_out.shape[0]
    flat_out = head_out.reshape(1, batch_rows, -1)
    blocks = out_proj.reshape(head_count, -1, out_proj.shape[1])
    shard_piece = lax.all_gather(flat_out, ("rep", "head"), axis=0, tiled=True)
    head_block = jnp.arange(shard_piece.shape[0], dtype=jnp.int32) % head_count
    chosen = jnp.take(blocks, head_block, axis=0)
    projected = jnp.einsum("kbf,kfc->kbc", shard_piece, chosen, preferred_element_type=jnp.float32)
    attended = (
        projected.reshape(rep_count, head_count, batch_rows, -1)
        .sum(axis=1)
        .reshape(rep_count * batch_rows, -1)
    )
    combined = residual.astype(jnp.float32) + attended
    scaled = combined * norm_gain.astype(jnp.float32)[None, :]
    logit_table = jnp.dot(scaled, centroid.astype(jnp.float32).T, precision=lax.Precision.HIGHEST)
    partial_logit = jnp.take_along_axis(logit_table, expert_ids, axis=1)
    squares, logit_total_sum = lax.psum(
        (jnp.sum(combined * combined, axis=1), partial_logit), ("rep", "head")
    )
    root_mean = jnp.sqrt(squares / D + 1e-06)[:, None]
    normed = (scaled / root_mean).astype(jnp.bfloat16)
    affinity = jax.nn.sigmoid(logit_total_sum / root_mean)
    weight_share = 2.5 * affinity / jnp.sum(affinity, axis=1, keepdims=True)
    experts = centroid.shape[0]
    pair_count = expert_ids.shape[0] * expert_ids.shape[1]
    capacity = 2 * pair_count // experts
    pair_expert, pair_slot = expert_slots(expert_ids, experts)
    slot_token = (
        jnp.zeros((experts, capacity), jnp.int32)
        .at[pair_expert, pair_slot]
        .set(jnp.arange(pair_count, dtype=jnp.int32) // expert_ids.shape[1])
    )
    outbound_rows = jnp.take(normed, slot_token, axis=0)
    expert_rows = lax.all_to_all(
        outbound_rows, ("rep", "head"), split_axis=0, concat_axis=2, tiled=True
    )[0]
    inner_act = jnp.dot(expert_rows, up_weight[0], preferred_element_type=jnp.float32)
    hidden = jax.nn.silu(inner_act).astype(jnp.bfloat16)
    result = jnp.dot(hidden, down_weight[0], preferred_element_type=jnp.float32).astype(
        jnp.bfloat16
    )
    returned = lax.all_to_all(
        result[None], ("rep", "head"), split_axis=2, concat_axis=0, tiled=True
    )
    gathered = (
        returned[pair_expert, pair_slot]
        .astype(jnp.float32)
        .reshape(expert_ids.shape[0], expert_ids.shape[1], -1)
    )
    routed_expert_sum = jnp.sum(weight_share[:, :, None] * gathered, axis=1)
    return (combined + routed_expert_sum).astype(jnp.bfloat16)


def solution(mesh):
    return jax.shard_map(
        per_device,
        mesh=mesh,
        in_specs=(
            P("rep", "head", None),
            P("rep", None, None),
            P(None, ("rep", "head"), None),
            P(),
            P(),
            P("head", None, None),
            P("head", None, None),
            P(None, ("rep", "head")),
            P(None, ("rep", "head")),
            P(("rep", "head")),
            P(None, ("rep", "head")),
            P(),
            P(("rep", "head"), None, None),
            P(("rep", "head"), None, None),
        ),
        out_specs=P(None, ("rep", "head")),
        check_vma=False,
    )
```

profile of v0, /device:TPU:1, one launch (start us, length us, event | category | flops | bytes accessed | tf_op | source)
XLA Modules:
  0.0 350.1 jit_solution(3712543610138085334)
XLA Ops:
  8.1 1.9 gather_fusion
  10.2 2.2 broadcast_in_dim.96
  12.4 11.9 %all-to-all-start = ((bf16[128,24,576]{2,1,0:T(8,128)(2,1)}), bf16[128,24,576]{2,1,0:T(8,128)(2,1)}, u32[]{:S(2)}, u32[]{:S(2)}) async-start(bf16[128,24,576]{2,1,0:T(8,128)(2,1)} %bitcast.87), calls=%async_computation | async-start | bytes 7864320 | tf_op jit(solution)/shard_map/all_to_all | solution.py:76
  27.4 3.3 fusion.70
  30.7 3.4 fusion.27
  34.1 40.6 %all-to-all-done = bf16[128,24,576]{2,1,0:T(8,128)(2,1)} async-done(((bf16[128,24,576]{2,1,0:T(8,128)(2,1)}), bf16[128,24,576]{2,1,0:T(8,128)(2,1)}, u32[]{:S(2)}, u32[]{:S(2)}) %all-to-all-start) | async-done | bytes 3538976 | tf_op jit(solution)/shard_map/all_to_all | solution.py:76
  74.7 3.3 fusion.69
  78.2 2.6 fusion.34
  84.2 1.1 copy-done.2
  85.4 1.5 add_add_fusion
  87.2 1.5 fusion.24
  88.9 9.2 %scatter_custom_fusion.1 = s32[4608]{0:T(1024)S(1)} fusion(s32[2304]{0:T(1024)S(1)} %get-tuple-element.37, s32[2304]{0:T(1024)S(1)} %get-tuple-element.36, s32[]{:T(128)} %constant.129.clone.1), kind=kCustom, calls=%fused_computation.95 | custom fusion | bytes 18436
  98.5 7.7 %gather_fusion.1 = bf16[128,2048,28]{1,2,0:T(8,128)(2,1)} fusion(bf16[4,2048,28]{1,2,0:T(8,128)(2,1)S(1)} %copy.99, s32[1024]{0:T(1024)S(1)} %pad_clamp_fusion.1), kind=kCustom, calls=%fused_computation.1 | custom fusion | bytes 29360640 | tf_op jit(solution)/shard_map/jit(_take)/gather | solution.py:99
  106.3 42.4 %all-gather.2.cloned.1.call-done = bf16[128,9,2048]{2,1,0:T(8,128)(2,1)} async-done(((bf16[1,9,2048]{2,1,0:T(8,128)(2,1)}), bf16[128,9,2048]{2,1,0:T(8,128)(2,1)}) %all-gather.2.cloned.1.call-update) | async-done | bytes 4718608 | tf_op jit(solution)/shard_map/all_gather | solution.py:97
  148.6 10.7 %bitcast_reduce_fusion = f32[32,9,28]{2,1,0:T(8,128)S(1)} fusion(bf16[128,9,2048]{2,1,0:T(8,128)(2,1)} %all-gather.2.cloned.1.call-done, bf16[128,2048,28]{1,2,0:T(8,128)(2,1)} %gather_fusion.1, pred[128]{0:T(512)(128)(4,1)S(1)} %compare_and_fusion.1), kind=kOutput, calls=%fused_computation.43 | convolution fusion | flops 139484800 | bytes 19431040 | tf_op jit(solution)/shard_map/kbf,kfc->kbc/dot_general | solution.py:100
  159.8 13.8 %gather_fusion.4 = f32[2304]{0:T(1024)S(1)} fusion(f32[288,128]{1,0:T(8,128)S(1)} %fusion.46, s32[2304]{0:T(1024)S(1)} %reshape.260), kind=kCustom, calls=%fused_computation.4 | custom fusion | bytes 36864 | tf_op jit(solution)/shard_map/jit(take_along_axis)/gather | solution.py:109
  173.8 62.9 %all-reduce = (f32[288]{0:T(512)S(1)}, f32[288,8]{0,1:T(8,128)S(1)}) all-reduce(f32[288]{0:T(512)S(1)} %multiply_reduce_fusion, f32[288,8]{0,1:T(8,128)S(1)} %and_select_fusion), channel_id=1, replica_groups=mesh['rep'=32,'head'=4] {'rep','head'}, use_global_device_ids=true, to_apply=%region_8.9 | all-reduce | flops 2592 | bytes 20736 | tf_op jit(solution)/shard_map/psum | solution.py:110
  236.8 8.8 %gather_fusion.2 = bf16[4608,28]{1,0:T(8,128)(2,1)S(1)} fusion(bf16[288,28]{1,0:T(8,128)(2,1)S(1)} %divide_convert_fusion.2, s32[5120]{0:T(1024)S(1)} %pad_clamp_fusion), kind=kCustom, calls=%fused_computation.2 | custom fusion | bytes 534528 | tf_op jit(solution)/shard_map/jit(_take)/gather | solution.py:126
  246.1 2.4 reshape.247
  249.2 1.2 reshape.295
  250.5 16.3 %all_to_all.38 = bf16[128,2,504]{2,1,0:T(2,128)(2,1)S(1)} all-to-all(bf16[128,2,504]{2,1,0:T(2,128)(2,1)S(1)} %reshape.295), channel_id=1, replica_groups=mesh['rep'=32,'head'=4] {'rep','head'}, dimensions={0} | all-to-all | bytes 516096 | tf_op jit(solution)/shard_map/all_to_all | solution.py:127
  266.8 1.4 reshape.296
  268.7 7.9 %fusion.12 = bf16[1,36,3584]{2,1,0:T(8,128)(2,1)S(1)} fusion(bf16[1,1024,3584]{2,1,0:T(8,128)(2,1)} %param.27, bf16[36,3584]{0,1:T(8,128)(2,1)S(1)} %reshape.289, bf16[1,3584,1024]{2,1,0:T(8,128)(2,1)} %param.26), kind=kOutput, calls=%fused_computation.17 | convolution fusion | flops 528795648 | bytes 15196160 | tf_op jit(solution)/shard_map/dot_general | solution.py:132
  276.6 2.5 copy.113
  279.6 19.7 %reduce.6 = bf16[3584,36]{1,0:T(8,128)(2,1)S(1)} reduce(bf16[3584,1,36]{2,1,0:T(2,128)(2,1)S(1)} %bitcast.88, bf16[]{:T(256)} %broadcast.298), dimensions={1}, to_apply=%bitcast.70.reduce_sub_computation | reduce | bytes 516098
  299.3 1.5 reshape.297
  300.8 3.9 %all-to-all-start.2 = ((bf16[128,2,504]{2,1,0:T(2,128)(2,1)}), bf16[128,2,504]{2,1,0:T(2,128)(2,1)S(1)}, u32[]{:S(2)}, u32[]{:S(2)}) async-start(bf16[128,2,504]{2,1,0:T(2,128)(2,1)} %reshape.297), calls=%async_computation.2 | async-start | bytes 524288 | tf_op jit(solution)/shard_map/all_to_all | solution.py:135
  305.5 10.5 %all-to-all-done.2 = bf16[128,2,504]{2,1,0:T(2,128)(2,1)S(1)} async-done(((bf16[128,2,504]{2,1,0:T(2,128)(2,1)}), bf16[128,2,504]{2,1,0:T(2,128)(2,1)S(1)}, u32[]{:S(2)}, u32[]{:S(2)}) %all-to-all-start.2) | async-done | bytes 258080 | tf_op jit(solution)/shard_map/all_to_all | solution.py:135
  316.9 3.1 copy.114
  320.0 4.0 %all_to_all.32 = bf16[1,36,128,28]{3,2,1,0:T(8,128)(2,1)S(1)} reshape(bf16[1,36,3584]{2,1,0:T(8,128)(2,1)} %copy.114) | data formatting | bytes 516096 | tf_op jit(solution)/shard_map/all_to_all | solution.py:135
  324.1 16.8 %gather_fusion.3 = bf16[2304,28]{1,0:T(8,128)(2,1)} fusion(bf16[128,36,28]{2,0,1:T(8,128)(2,1)S(1)} %bitcast.86, s32[2304]{0:T(1024)S(1)} %get-tuple-element.29), kind=kCustom, calls=%fused_computation.3 | custom fusion | bytes 276480 | tf_op jit(solution)/shard_map/gather | solution.py:139
  340.9 1.5 fusion.23
  (97 shorter events, 13.2 us)
Async XLA Ops:
  6.5 20.4 %copy-start = (bf16[16,128,512]{2,1,0:T(8,128)(2,1)S(1)}, bf16[16,128,512]{2,1,0:T(8,128)(2,1)}, u32[]{:S(2)}) copy-start(bf16[16,128,512]{2,1,0:T(8,128)(2,1)} %param.19) | copy-start | bytes 6291460
  12.4 13.2 %copy-start.10 = (s32[32]{0:T(128)S(1)}, s32[32]{0:T(128)}, u32[]{:S(2)}) copy-start(s32[32]{0:T(128)} %param.18) | copy-start | bytes 388
  12.4 13.9 %slice-start.1 = ((bf16[9,16,192]{2,1,0:T(8,128)(2,1)}), bf16[9,16,64]{2,1,0:T(8,128)(2,1)S(1)}, s32[]{:S(2)}) async-start(bf16[9,16,192]{2,1,0:T(8,128)(2,1)} %param.14), calls=%async_computation.5 | async-start | bytes 73728 | tf_op jit(solution)/shard_map/slice | solution.py:73
  12.4 14.6 %slice-start = ((bf16[9,16,192]{2,1,0:T(8,128)(2,1)}), bf16[9,16,128]{2,1,0:T(8,128)(2,1)S(1)}, s32[]{:S(2)}) async-start(bf16[9,16,192]{2,1,0:T(8,128)(2,1)} %param.14), calls=%async_computation.4 | async-start | bytes 73728 | tf_op jit(solution)/shard_map/slice | solution.py:71
  12.4 62.3 %all-to-all-start = ((bf16[128,24,576]{2,1,0:T(8,128)(2,1)}), bf16[128,24,576]{2,1,0:T(8,128)(2,1)}, u32[]{:S(2)}, u32[]{:S(2)}) async-start(bf16[128,24,576]{2,1,0:T(8,128)(2,1)} %bitcast.87), calls=%async_computation | async-start | bytes 7864320 | tf_op jit(solution)/shard_map/all_to_all | solution.py:76
  24.3 124.3 %all-gather.2.cloned.1.call-start = ((), (), s32[]{:S(2)}) async-start(), calls=%async_computation.3 | async-start | bytes 8454144 | tf_op jit(solution)/shard_map/all_gather | solution.py:97
  78.2 2.6 copy-start.3
  80.9 1.2 copy-start.5
  80.9 1.7 copy-start.4
  81.3 1.8 copy-start.6
  81.3 2.0 copy-start.11
  84.2 1.2 copy-start.2
  86.9 1.8 copy-start.8
  86.9 1.9 copy-start.9
  106.3 53.3 %copy-start.7 = (bf16[128,28]{0,1:T(8,128)(2,1)S(1)}, bf16[128,28]{0,1:T(8,128)(2,1)}, u32[]{:S(2)}) copy-start(bf16[128,28]{0,1:T(8,128)(2,1)} %param.24) | copy-start | bytes 21508
  300.8 15.2 %all-to-all-start.2 = ((bf16[128,2,504]{2,1,0:T(2,128)(2,1)}), bf16[128,2,504]{2,1,0:T(2,128)(2,1)S(1)}, u32[]{:S(2)}, u32[]{:S(2)}) async-start(bf16[128,2,504]{2,1,0:T(2,128)(2,1)} %reshape.297), calls=%async_computation.2 | async-start | bytes 524288 | tf_op jit(solution)/shard_map/all_to_all | solution.py:135
  324.1 19.2 %copy-start.1 = (bf16[16,128,512]{2,1,0:T(8,128)(2,1)S(1)}, bf16[16,128,512]{2,1,0:T(8,128)(2,1)}, u32[]{:S(2)}) copy-start(bf16[16,128,512]{2,1,0:T(8,128)(2,1)} %param.19) | copy-start | bytes 6291460
Sparse Core Ops, SparseCore 0:
  82.2 66.4 all-gather.1
where the time goes:
time: 351 us; the launch traced here: 350 us
  waiting for transfers between devices  93.4 us (27%)
  local copies, waits for them, and re-layouts  87.3 us (25%)
  blocking collectives  79.3 us (23%)
  matrix products  32.2 us (9%)
  other arithmetic  26.8 us (8%)
  starting transfers between devices  15.8 us (5%)
  between operations  15.2 us (4%)
    psum x1, blocking collectives, per_device(): lax.psum((jnp.sum(combined * combined, axis=1), partial_logit), ('rep', '...  62.9 us
    all_gather x1, waiting for transfers between devices, per_device(): shard_piece = lax.all_gather(flat_out, ('rep', 'head'), axis=0, tiled=True)  42.4 us
    all_to_all x1, waiting for transfers between devices, per_device(): lax.all_to_all(copies, ('rep', 'head'), split_axis=0, concat_axis=0, tile...  40.6 us
    unnamed x3, other arithmetic  19.9 us
    gather x1, local copies, waits for them, and re-layouts, per_device(): returned[pair_expert, pair_slot].astype(jnp.float32)  16.8 us
    all_to_all x1, blocking collectives, per_device(): lax.all_to_all(outbound_rows, ('rep', 'head'), split_axis=0, concat_axis=...  16.3 us
    unnamed x33, local copies, waits for them, and re-layouts  16.2 us
    gather x5, local copies, waits for them, and re-layouts, per_device(): partial_logit = jnp.take_along_axis(logit_table, expert_ids, axis=1)  14.2 us
  transfers between devices with their start and end apart: 3, of which 3 were waited for; matrix products, arithmetic and copies ran while one was open for 9% of the time, Pallas kernels for 0%

commit v1 on v0

v1 whole, which is shorter than its diff:
```python
import functools
import math
import types

import jax
import jax.numpy as jnp
from jax import lax
from jax.experimental import pallas as pl
from jax.experimental.pallas import tpu as pltpu
from jax.sharding import PartitionSpec as P

MESH = pl.DeviceIdType.MESH
F32 = jnp.float32
BF16 = jnp.bfloat16
RES = 8
SLOTS = 40
CORES = 2


def nn(a, b):
    return lax.dot_general(a, b, (((1,), (0,)), ((), ())), preferred_element_type=F32)


def nt(a, b):
    return lax.dot_general(a, b, (((1,), (1,)), ((), ())), preferred_element_type=F32)


def one_hot(mask):
    return jnp.where(mask, 1.0, 0.0).astype(BF16)


def iota(shape, dim):
    return lax.broadcasted_iota(jnp.int32, shape, dim)


def split2(value):
    high = value.astype(BF16).astype(F32)
    return high, (value - high).astype(BF16).astype(F32)


def layer_kernel(names, dims, *refs):
    (
        source_ref, length_ref, query_hbm, cache_hbm, moved_hbm, absorb_hbm, value_hbm, outproj_hbm,
        residual_hbm, gain_hbm, centroid_hbm, ids_hbm, up_hbm, down_hbm, out_ref,
    ) = refs[:15]
    s = types.SimpleNamespace(**dict(zip(names, refs[15:])))
    reps, heads, lines, xs, zs, groups, moved_n, columns, tokens, features = dims
    line_columns = columns * CORES * heads
    width = -(-line_columns // 128) * 128
    pitch = -(-columns // 16) * 16
    batch = tokens // reps
    half = lines * batch
    head_rows = batch * 16
    kv = value_hbm.shape[1]
    nope = absorb_hbm.shape[1]
    qdim = query_hbm.shape[1]
    rope = qdim - nope
    full = kv + rope
    head_features = 16 * value_hbm.shape[2]
    scale = 1.0 / math.sqrt(qdim)

    rep = lax.axis_index("rep")
    head = lax.axis_index("head")
    line = rep // CORES
    core = rep % CORES
    lx = line // zs
    lz = line % zs
    owner = core * heads + head

    def rep_at(dx, dz, dc):
        return (((lx + dx) % xs) * zs + (lz + dz) % zs) * CORES + (core + dc) % CORES

    def line_at(dx, dz):
        return ((lx + dx) % xs) * zs + (lz + dz) % zs

    line_offsets = [(dx, dz) for dx in range(xs) for dz in range(zs) if (dx, dz) != (0, 0)]
    line_offsets.sort(key=lambda o: -(min(o[0], xs - o[0]) + min(o[1], zs - o[1])))
    plane_offsets = [(dx, dz, dc) for dx, dz in line_offsets for dc in range(CORES)]
    plane_offsets += [(0, 0, dc) for dc in range(1, CORES)]

    def load(src, dst, sem):
        copy = pltpu.make_async_copy(src, dst, s.load_sem.at[sem])
        copy.start()
        return copy

    load_moved = load(moved_hbm, s.moved, 0)
    load_query = load(query_hbm, s.query, 1)
    load_absorb = load(absorb_hbm, s.absorb, 2)
    load_outproj = load(outproj_hbm, s.outproj, 3)
    load_residual = load(residual_hbm, s.residual, 4)
    load_gain = load(gain_hbm, s.gain, 5)
    load_centroid = load(centroid_hbm, s.centroid, 6)
    load_ids = load(ids_hbm, s.ids, 7)
    load_cache = load(cache_hbm, s.cache, 8)
    load_value = load(value_hbm, s.value, 9)
    load_up = load(up_hbm, s.up, 10)
    chunk = zs * line_columns
    load_down = [load(down_hbm.at[:, pl.ds(i * chunk, chunk)], s.down.at[i], 11 + i) for i in range(xs)]

    barrier = pltpu.get_barrier_semaphore()
    partners = [(rep_at(*o), head) for o in plane_offsets]
    for dh in range(1, heads):
        for dc in range(CORES):
            partners.append((rep_at(0, 0, dc), (head + dh) % heads))
    for partner in partners:
        pl.semaphore_signal(barrier, inc=1, device_id=partner, device_id_type=MESH)

    load_moved.wait()
    for g in range(groups):
        s.moved_out[g] = s.moved[source_ref[g]]
    s.moved_in[rep] = s.moved_out[rep]

    load_outproj.wait()
    pad = jnp.zeros((pitch - columns, 512), F32)
    for i in range(outproj_hbm.shape[1] // 512):
        cut = s.outproj[:, pl.ds(512 * i, 512)].astype(F32)
        s.cols_out[:, pl.ds(512 * i, 512)] = jnp.concatenate([cut, pad], axis=0).astype(BF16)
    for copy in (load_residual, load_gain, load_centroid, load_ids):
        copy.wait()
    tok_lanes = -(-tokens // 128) * 128
    experts = centroid_hbm.shape[1]
    exp_lanes = -(-experts // 128) * 128
    s.static_out[...] = jnp.zeros_like(s.static_out)

    def padded(value):
        return jnp.concatenate([value.astype(F32), jnp.zeros((pitch - columns, value.shape[1]), F32)], axis=0).astype(BF16)

    s.static_out[:, pl.ds(0, tokens)] = padded(s.residual[...])
    s.static_out[:, pl.ds(tok_lanes, experts)] = padded(s.centroid[...])
    gain_row = jnp.broadcast_to(s.gain[...].astype(F32), (pitch, columns))
    diagonal = iota((pitch, columns), 0) == iota((pitch, columns), 1)
    gain_col = jnp.sum(jnp.where(diagonal, gain_row, 0.0), axis=1, keepdims=True)
    first_lane = iota((pitch, 128), 1) == 0
    s.static_out[:, pl.ds(tok_lanes + exp_lanes, 128)] = jnp.where(first_lane, gain_col, 0.0).astype(BF16)

    pl.semaphore_wait(barrier, len(partners))

    def push(src, dst, phase, k, to_rep, to_head):
        copy = pltpu.make_async_remote_copy(
            src_ref=src, dst_ref=dst, send_sem=phase.at[0, k], recv_sem=phase.at[1, k],
            device_id=(to_rep, to_head), device_id_type=MESH,
        )
        copy.start()
        return copy

    started = []
    rows_copies = []
    for k, offset in enumerate(plane_offsets):
        to_rep = rep_at(*offset)
        rows_copies.append(push(s.moved_out.at[to_rep], s.moved_in.at[rep], s.rows_sem, k, to_rep, head))

    own_rows = pl.ds(pl.multiple_of(owner * pitch, pitch), pitch)
    cols_copies = []
    static_copies = []
    for dh in range(1, heads):
        to_head = (head + dh) % heads
        lanes = pl.ds(pl.multiple_of(to_head * head_features, 128), head_features)
        cols_copies.append(push(s.cols_out.at[:, lanes], s.cols_in.at[own_rows], s.cols_sem, dh - 1, rep, to_head))
        static_copies.append(push(s.static_out, s.static_in.at[own_rows], s.static_sem, dh - 1, rep, to_head))
    own_lanes = pl.ds(pl.multiple_of(head * head_features, 128), head_features)
    own_cols = pltpu.make_async_copy(s.cols_out.at[:, own_lanes], s.cols_in.at[own_rows], s.load_sem.at[11 + xs])
    own_cols.start()
    own_static = pltpu.make_async_copy(s.static_out, s.static_in.at[own_rows], s.load_sem.at[12 + xs])
    own_static.start()

    load_query.wait()
    s.query_f[...] = s.query[:, pl.ds(0, nope)].astype(F32)
    s.joined[kv // 128, :, pl.ds(0, rope)] = s.query[:, pl.ds(nope, rope)].astype(F32)
    load_absorb.wait()
    for h in range(16):
        part = s.query_f[pl.ds(h, batch, stride=16), :].astype(BF16)
        absorbed = nn(part, s.absorb[h])
        for i in range(kv // 128):
            s.joined[i, pl.ds(h, batch, stride=16), :] = absorbed[:, 128 * i:128 * i + 128]

    def joined_query(i):
        parts = [s.joined[j, pl.ds(16 * i, 16), :] for j in range(kv // 128)]
        parts.append(s.joined[kv // 128, pl.ds(16 * i, 16), pl.ds(0, rope)])
        return jnp.concatenate(parts, axis=1).astype(BF16)

    def keep_latents(i, value):
        for j in range(kv // 128):
            s.latents[j, pl.ds(16 * i, 16), :] = value[:, 128 * j:128 * j + 128]

    s.far_query[...] = joined_query(RES)
    query_copies = []
    for dh in range(1, heads):
        query_copies.append(push(s.far_query, s.far_queries.at[head], s.query_sem, dh - 1, rep, (head + dh) % heads))
    s.far_queries[head] = s.far_query[...]

    load_cache.wait()
    for i in range(RES):
        scores = nn(joined_query(i), s.cache[i]) * scale
        weights = jnp.exp(scores - jnp.max(scores, axis=1, keepdims=True))
        weights = (weights / jnp.sum(weights, axis=1, keepdims=True)).astype(BF16)
        keep_latents(i, nt(weights, s.cache[i, pl.ds(0, kv), :]))

    for copy in cols_copies + static_copies:
        copy.wait_recv()
    own_cols.wait()
    own_static.wait()
    core_rows = pl.ds(pl.multiple_of(core * (heads * pitch), heads * pitch), heads * pitch)
    other = rep_at(0, 0, 1)
    cols_pass = push(s.cols_in.at[core_rows], s.cols_in.at[core_rows], s.cols_sem, heads - 1, other, head)
    static_pass = push(s.static_in.at[core_rows], s.static_in.at[core_rows], s.static_sem, heads - 1, other, head)

    row_count = reps * moved_n
    s.rows_f[pl.ds(pl.multiple_of(rep * moved_n, moved_n), moved_n), :] = s.moved_in[rep].astype(F32)
    for copy, (dx, dz, dc) in zip(rows_copies, plane_offsets):
        copy.wait_recv()
        from_rep = rep_at(-dx, -dz, -dc)
        s.rows_f[pl.ds(pl.multiple_of(from_rep * moved_n, moved_n), moved_n), :] = s.moved_in[from_rep].astype(F32)
    s.rows_b[...] = s.rows_f[...].astype(BF16)
    for copy in query_copies:
        copy.wait_recv()
    far_all = jnp.concatenate([s.far_queries[h] for h in range(heads)], axis=0)
    far_scores = nt(far_all, s.rows_b[...]) * scale
    place = iota((1, row_count), 1)
    from_device = (place * 2731) >> 16
    position = place + from_device * (moved_n * (heads - 1)) + head * moved_n
    far_scores = jnp.where(position < length_ref[rep], far_scores, -1e30)
    far_max = jnp.max(far_scores, axis=1, keepdims=True)
    far_weights = jnp.exp(far_scores - far_max)
    far_sum = jnp.sum(far_weights, axis=1, keepdims=True)
    s.far_out[:, pl.ds(0, kv)] = nn(far_weights.astype(BF16), s.rows_b[:, pl.ds(0, kv)])
    lane = iota((heads * 16, 128), 1)
    s.far_out[:, pl.ds(kv, 128)] = jnp.where(lane == 0, far_max, jnp.where(lane == 1, far_sum, 0.0))
    far_copies = []
    for dh in range(1, heads):
        to_head = (head + dh) % heads
        their_rows = pl.ds(pl.multiple_of(to_head * 16, 16), 16)
        far_copies.append(push(s.far_out.at[their_rows], s.far_in.at[head], s.far_sem, dh - 1, rep, to_head))
    s.far_in[head] = s.far_out[pl.ds(pl.multiple_of(head * 16, 16), 16), :]
    load_value.wait()
    for copy in far_copies:
        copy.wait_recv()
    top = s.far_in[0, :, pl.ds(kv, 1)]
    for h in range(1, heads):
        top = jnp.maximum(top, s.far_in[h, :, pl.ds(kv, 1)])
    total = jnp.zeros((16, kv), F32)
    weight_sum = jnp.zeros((16, 1), F32)
    for h in range(heads):
        factor = jnp.exp(s.far_in[h, :, pl.ds(kv, 1)] - top)
        total = total + factor * s.far_in[h, :, pl.ds(0, kv)]
        weight_sum = weight_sum + factor * s.far_in[h, :, pl.ds(kv + 1, 1)]
    keep_latents(RES, total / weight_sum)

    for h in range(16):
        parts = [s.latents[i, pl.ds(h, batch, stride=16), :] for i in range(kv // 128)]
        part = jnp.concatenate(parts, axis=1).astype(BF16)
        s.heads_f[pl.ds(h, batch, stride=16), :] = nn(part, s.value[h])
    s.heads_out[...] = s.heads_f[...].astype(BF16)
    head_copies = []
    for k, (dx, dz) in enumerate(line_offsets):
        head_copies.append(push(s.heads_out, s.heads_in.at[line], s.heads_sem, k, rep_at(dx, dz, 0), head))
    s.heads_in[line] = s.heads_out[...]

    cols_pass.wait_recv()
    static_pass.wait_recv()
    row = iota((width, width), 0)
    col = iota((width, width), 1)
    squeeze = one_hot((row < line_columns) & (col == row + (pitch - columns) * ((row * 2341) >> 16)))
    for i in range(head_features // 512):
        cut = pl.ds(512 * i, 512)
        s.cols[:, cut] = nn(squeeze, s.cols_in[:, cut]).astype(BF16)
    static = nn(squeeze, s.static_in[...]).astype(BF16)
    held = iota((tokens, tokens), 0)
    held_core = jnp.where(held >= half, 1, 0)
    held_line = ((held - half * held_core) * 7282) >> 16
    order = held - half * held_core + batch * (held_line + held_core)
    reorder = one_hot(iota((tokens, tokens), 1) == order)
    s.reorder[...] = reorder
    s.residual_c[...] = nt(reorder, static[:, :tokens])
    their_expert = iota((lines, experts), 0) * (CORES * heads) + owner
    pick = one_hot(iota((lines, experts), 1) == their_expert)
    s.centroid_c[...] = nt(pick, static[:, tok_lanes:tok_lanes + experts])
    first = one_hot((iota((8, 128), 0) == 0) & (iota((8, 128), 1) == 0))
    s.gain_c[...] = nt(first, static[:, tok_lanes + exp_lanes:])
    named = jnp.zeros((lines, tokens), F32)
    my_experts = iota((lines, tokens), 0) * (CORES * heads) + owner
    for k in range(ids_hbm.shape[0]):
        named = jnp.where(my_experts == s.ids[pl.ds(k, 1), :], 1.0, named)
    earlier = one_hot(iota((tokens, tokens), 0) < iota((tokens, tokens), 1))
    slot = jnp.where(named > 0.0, nn(named.astype(BF16), earlier), -1.0)
    slot_index = iota((SLOTS, tokens), 0).astype(F32)
    pieces = [jnp.where(slot[e:e + 1, :] == slot_index, 1.0, 0.0) for e in range(lines)]
    s.gather[...] = jnp.concatenate(pieces, axis=0).astype(BF16)
    s.gather_held[...] = nt(s.gather[...], reorder).astype(BF16)
    eye = one_hot(iota((tokens, tokens), 0) == iota((tokens, tokens), 1))
    s.scatter[...] = nt(eye, s.gather[...]).astype(BF16)

    s.heads_w[pl.ds(pl.multiple_of(line * head_rows, head_rows), head_rows), :] = s.heads_in[line].astype(F32)
    for copy, (dx, dz) in zip(head_copies, line_offsets):
        copy.wait_recv()
        from_line = line_at(-dx, -dz)
        s.heads_w[pl.ds(pl.multiple_of(from_line * head_rows, head_rows), head_rows), :] = s.heads_in[from_line].astype(F32)
    acts = [s.heads_w[pl.ds(h, half, stride=16), :].astype(BF16) for h in range(16)]
    partial = nt(jnp.concatenate(acts, axis=1), s.cols[...])
    s.sum_out[...] = partial.astype(BF16)
    sum_copies = []
    for dh in range(1, heads):
        sum_copies.append(push(s.sum_out, s.sum_in.at[dh - 1], s.sum_sem, dh - 1, rep, (head + dh) % heads))
    for dh, copy in enumerate(sum_copies):
        copy.wait_recv()
        partial = partial + s.sum_in[dh].astype(F32)
    s.swap_out[...] = partial
    swap = push(s.swap_out, s.swap_in, s.swap_sem, 0, other, head)
    swap.wait_recv()
    mine, theirs = s.swap_out[...], s.swap_in[...]
    first_core = core == 0
    attended = jnp.concatenate([jnp.where(first_core, mine, theirs), jnp.where(first_core, theirs, mine)], axis=0)
    combined = s.residual_c[...] + attended
    s.combined[...] = combined

    square_high, square_low = split2(jnp.sum(combined * combined, axis=1, keepdims=True))
    scaled = combined * s.gain_c[0:1, :]
    token_lane = iota((tokens, width), 1)
    scaled = jnp.where(token_lane == line_columns, square_high, scaled)
    scaled = jnp.where(token_lane == line_columns + 1, square_low, scaled)
    gathered = nn(s.gather_held[...], scaled.astype(BF16))
    slot_lane = iota((SLOTS, width), 1)
    for e in range(lines):
        rows = gathered[SLOTS * e:SLOTS * e + SLOTS]
        high, low = split2(jnp.sum(rows * s.centroid_c[e:e + 1, :], axis=1, keepdims=True))
        rows = jnp.where(slot_lane == line_columns + 2, high, rows)
        rows = jnp.where(slot_lane == line_columns + 3, low, rows)
        s.tok_out[e] = rows.astype(BF16)
    tok_copies = []
    for k, (dx, dz) in enumerate(line_offsets):
        tok_copies.append(push(s.tok_out.at[line_at(dx, dz)], s.tok_in.at[line], s.tok_sem, k, rep_at(dx, dz, 0), head))
    s.tok_in[line] = s.tok_out[line]

    rest = combined
    my_columns = one_hot((iota((pitch, width), 0) < columns) & (iota((pitch, width), 1) == owner * columns + iota((pitch, width), 0)))
    combined_own = jnp.zeros((pitch, tokens), F32)
    for _ in range(3):
        part = rest.astype(BF16)
        rest = rest - part.astype(F32)
        combined_own = combined_own + nn(nt(my_columns, part).astype(BF16), s.reorder[...])
    s.combined_own[...] = combined_own

    load_up.wait()
    inner = nn(s.tok_in[line][:, :line_columns], s.up[line])
    stats = s.tok_in[line].astype(F32)[:, width - 128:]
    for copy, (dx, dz) in zip(tok_copies, line_offsets):
        copy.wait_recv()
        from_line = line_at(-dx, -dz)
        rows = s.tok_in[from_line]
        inner = inner + nn(rows[:, :line_columns], s.up[from_line])
        stats = stats + rows.astype(F32)[:, width - 128:]
    at = line_columns - (width - 128)
    squares = stats[:, at:at + 1] + stats[:, at + 1:at + 2]
    logit = stats[:, at + 2:at + 3] + stats[:, at + 3:at + 4]
    root_mean = jnp.sqrt(squares / features + 1e-6)
    inner = inner / root_mean
    hidden = (inner * jax.nn.sigmoid(inner)).astype(BF16)
    affinity = jax.nn.sigmoid(logit / root_mean)
    affinity_high, affinity_low = split2(affinity)
    for copy in load_down:
        copy.wait()
    back_copies = []
    filler = jnp.zeros((SLOTS, width - line_columns), F32)
    x_order = sorted(range(xs), key=lambda dx: -min(dx, xs - dx))
    for dx in x_order:
        to_x = (lx + dx) % xs
        result = nn(hidden, s.down[to_x]) * affinity
        for z in range(zs):
            piece = jnp.concatenate([result[:, z * line_columns:(z + 1) * line_columns], filler], axis=1)
            piece = jnp.where(slot_lane == line_columns, affinity_high, piece)
            piece = jnp.where(slot_lane == line_columns + 1, affinity_low, piece)
            s.back_out[to_x * zs + z] = piece.astype(BF16)
        for dz in range(zs):
            if (dx, dz) != (0, 0):
                k = line_offsets.index((dx, dz))
                back_copies.append((k, push(s.back_out.at[line_at(dx, dz)], s.back_in.at[line], s.back_sem, k, rep_at(dx, dz, 0), head)))
    s.back_in[line] = s.back_out[line]
    for _, copy in back_copies:
        copy.wait_recv()

    returned = jnp.concatenate([s.back_in[e].astype(F32) for e in range(lines)], axis=0).astype(BF16)
    summed = nn(s.scatter[...], returned)
    share_high, share_low = split2(summed[:, line_columns:line_columns + 1] + summed[:, line_columns + 1:line_columns + 2])
    summed = jnp.where(token_lane == line_columns, share_high, summed)
    summed = jnp.where(token_lane == line_columns + 1, share_low, summed)
    place_in = row & (pitch - 1)
    wanted = jnp.where(place_in < columns, row - (pitch - columns) * (row // pitch), line_columns + place_in - columns)
    spread = one_hot((col == wanted) & (place_in < columns + 2))
    pieces = nt(spread, summed.astype(BF16)).astype(BF16)
    for j in range(CORES * heads):
        s.last_out[j] = pieces[pitch * j:pitch * j + pitch]
    last_copies = []
    k = 0
    for dc in range(CORES):
        for dh in range(heads):
            if (dc, dh) != (0, 0):
                to_core, to_head = (core + dc) % CORES, (head + dh) % heads
                last_copies.append(push(
                    s.last_out.at[to_core * heads + to_head], s.last_in.at[owner], s.last_sem, k, rep_at(0, 0, dc), to_head))
                k += 1
    s.last_in[owner] = s.last_out[owner]
    for copy in last_copies:
        copy.wait_recv()
    routed = s.last_in[0].astype(F32)
    for j in range(1, CORES * heads):
        routed = routed + s.last_in[j].astype(F32)
    share = routed[columns:columns + 1] + routed[columns + 1:columns + 2]
    layer_out = s.combined_own[...] + 2.5 * routed / share
    out_ref[...] = layer_out[:columns].astype(BF16)

    sends = rows_copies + cols_copies + static_copies + [cols_pass, static_pass] + query_copies + far_copies
    sends += head_copies + sum_copies + [swap] + tok_copies + [copy for _, copy in back_copies] + last_copies
    for copy in sends:
        copy.wait_send()


def per_device(
    query, latent_cache, moved_rows, target_group, moved_length, key_absorb, value_head_projection,
    out_proj, residual, norm_gain, centroid, expert_ids, up_weight, down_weight,
):
    reps = lax.axis_size("rep")
    heads = lax.axis_size("head")
    lines = reps // CORES
    xs = 4 if lines % 4 == 0 else lines
    zs = lines // xs
    groups, moved_n, full = moved_rows.shape
    batch, local_heads, qdim = query.shape
    columns = out_proj.shape[1]
    tokens, topk = expert_ids.shape
    features, hidden = up_weight.shape[1:]
    experts = centroid.shape[0]
    kv = value_head_projection.shape[1]
    vd = value_head_projection.shape[2]
    context = latent_cache.shape[1]
    line_columns = columns * CORES * heads
    width = -(-line_columns // 128) * 128
    pitch = -(-columns // 16) * 16
    half = tokens // CORES
    tok_lanes = -(-tokens // 128) * 128
    static_lanes = tok_lanes + -(-experts // 128) * 128 + 128
    head_features = local_heads * vd

    match = target_group[None, :] == jnp.arange(groups, dtype=jnp.int32)[:, None]
    source = jnp.sum(jnp.where(match, jnp.arange(groups, dtype=jnp.int32)[None, :], 0), axis=1)
    length = jnp.sum(jnp.where(match, moved_length[None, :], 0), axis=1)

    vmem = dict(
        moved=((groups, moved_n, full), BF16),
        moved_out=((groups, moved_n, full), BF16),
        moved_in=((reps, moved_n, full), BF16),
        rows_f=((reps * moved_n, full), F32),
        rows_b=((reps * moved_n, full), BF16),
        query=((batch * local_heads, qdim), BF16),
        query_f=((batch * local_heads, 128), F32),
        absorb=(key_absorb.shape, BF16),
        value=(value_head_projection.shape, BF16),
        cache=((latent_cache.shape[0], full, context), BF16),
        outproj=((columns, out_proj.shape[0]), BF16),
        cols_out=((pitch, out_proj.shape[0]), BF16),
        cols_in=((pitch * CORES * heads, head_features), BF16),
        cols=((width, head_features), BF16),
        residual=((columns, tokens), BF16),
        gain=((1, columns), BF16),
        centroid=((columns, experts), BF16),
        ids=((topk, tokens), jnp.int32),
        static_out=((pitch, static_lanes), BF16),
        static_in=((pitch * CORES * heads, static_lanes), BF16),
        residual_c=((tokens, width), F32),
        centroid_c=((lines, width), F32),
        gain_c=((8, width), F32),
        reorder=((tokens, tokens), BF16),
        gather=((lines * SLOTS, tokens), BF16),
        gather_held=((lines * SLOTS, tokens), BF16),
        scatter=((tokens, lines * SLOTS), BF16),
        joined=((kv // 128 + 1, batch * local_heads, 128), F32),
        latents=((kv // 128, batch * local_heads, 128), F32),
        heads_f=((batch * local_heads, vd), F32),
        heads_out=((batch * local_heads, vd), BF16),
        heads_in=((lines, batch * local_heads, vd), BF16),
        heads_w=((lines * batch * local_heads, vd), F32),
        far_query=((local_heads, full), BF16),
        far_queries=((heads, local_heads, full), BF16),
        far_out=((heads * local_heads, kv + 128), F32),
        far_in=((heads, local_heads, kv + 128), F32),
        sum_out=((half, width), BF16),
        sum_in=((heads - 1, half, width), BF16),
        swap_out=((half, width), F32),
        swap_in=((half, width), F32),
        combined=((tokens, width), F32),
        combined_own=((pitch, tokens), F32),
        tok_out=((lines, SLOTS, width), BF16),
        tok_in=((lines, SLOTS, width), BF16),
        up=((lines, line_columns, hidden), BF16),
        down=((xs, hidden, zs * line_columns), BF16),
        back_out=((lines, SLOTS, width), BF16),
        back_in=((lines, SLOTS, width), BF16),
        last_out=((CORES * heads, pitch, tokens), BF16),
        last_in=((CORES * heads, pitch, tokens), BF16),
    )
    sems = dict(
        load_sem=(13 + xs,), rows_sem=(2, reps - 1), cols_sem=(2, heads), static_sem=(2, heads),
        query_sem=(2, heads - 1), far_sem=(2, heads - 1), heads_sem=(2, lines - 1), sum_sem=(2, heads - 1),
        swap_sem=(2, 1), tok_sem=(2, lines - 1), back_sem=(2, lines - 1), last_sem=(2, CORES * heads - 1),
    )
    names = list(vmem) + list(sems)
    scratch = [pltpu.VMEM(shape, dtype) for shape, dtype in vmem.values()]
    scratch += [pltpu.SemaphoreType.DMA(shape) for shape in sems.values()]
    dims = (reps, heads, lines, xs, zs, groups, moved_n, columns, tokens, features)
    layer_out = pl.pallas_call(
        functools.partial(layer_kernel, names, dims),
        out_shape=jax.ShapeDtypeStruct((columns, tokens), BF16),
        in_specs=[pl.BlockSpec(memory_space=pltpu.SMEM)] * 2 + [pl.BlockSpec(memory_space=pl.ANY)] * 12,
        out_specs=pl.BlockSpec(memory_space=pltpu.VMEM),
        scratch_shapes=scratch,
        compiler_params=pltpu.CompilerParams(
            collective_id=0, has_side_effects=True, vmem_limit_bytes=60 * 1024 * 1024
        ),
        name="latent_moe_layer",
    )(
        source, length, query.reshape(batch * local_heads, qdim), jnp.swapaxes(latent_cache, 1, 2), moved_rows,
        key_absorb, value_head_projection, out_proj.T, residual.T, norm_gain.reshape(1, columns), centroid.T,
        expert_ids.T, up_weight.reshape(lines, line_columns, hidden), down_weight[0],
    )
    return layer_out.T


def solution(mesh):
    return jax.shard_map(
        per_device,
        mesh=mesh,
        in_specs=(
            P("rep", "head", None),
            P("rep", None, None),
            P(None, ("rep", "head"), None),
            P(),
            P(),
            P("head", None, None),
            P("head", None, None),
            P(None, ("rep", "head")),
            P(None, ("rep", "head")),
            P(("rep", "head")),
            P(None, ("rep", "head")),
            P(),
            P(("rep", "head"), None, None),
            P(("rep", "head"), None, None),
        ),
        out_specs=P(None, ("rep", "head")),
        check_vma=False,
    )
```

time: 351 us -> 70.6 us (0.20)
  waiting for transfers between devices: 93.4 us -> 0 us
  local copies, waits for them, and re-layouts: 87.3 us -> 1.35 us
  blocking collectives: 79.3 us -> 0 us
  Pallas kernels: 0 us -> 67.7 us
  matrix products: 32.2 us -> 0 us
  other arithmetic: 26.8 us -> 1.33 us
  starting transfers between devices: 15.8 us -> 0 us
  between operations: 15.2 us -> 0.01 us
    pallas_call x0 -> x1, Pallas kernels: none -> 67.7 us  [per_device(): pl.pallas_call(functools.partial(layer_kernel, names, dims), out_shape=ja...]
    psum x1 -> x0, blocking collectives: 62.9 us -> none  [per_device(): lax.psum((jnp.sum(combined * combined, axis=1), partial_logit), ('rep', '...]
    gather x11 -> x0, local copies, waits for them, and re-layouts: 52.3 us -> none  [the longest x1 16.8 us: per_device(): returned[pair_expert, pair_slot].astype(jnp.float32)]
    all_to_all x2 -> x0, waiting for transfers between devices: 51 us -> none  [the longest x1 40.6 us: per_device(): lax.all_to_all(copies, ('rep', 'head'), split_axis=0, concat_axis=0, tile...]
    all_gather x1 -> x0, waiting for transfers between devices: 42.4 us -> none  [per_device(): shard_piece = lax.all_gather(flat_out, ('rep', 'head'), axis=0, tiled=True)]
    dot_general x8 -> x0, matrix products: 29 us -> none  [the longest x1 10.7 us: per_device(): jnp.einsum('kbf,kfc->kbc', shard_piece, chosen, preferred_element_type=jn...]
    unnamed x3 -> x0, other arithmetic: 19.9 us -> none
    all_to_all x1 -> x0, blocking collectives: 16.3 us -> none  [per_device(): lax.all_to_all(outbound_rows, ('rep', 'head'), split_axis=0, concat_axis=...]
  transfers between devices with their start and end apart: 3 -> 0, of which waited for: 3 -> 0; matrix products, arithmetic and copies ran while one was open for 9% -> 0% of each run, Pallas kernels for 0% -> 0%
where the time goes in v1:
time: 70.6 us; the launch traced here: 70.4 us
  Pallas kernels  67.7 us (96%)
  local copies, waits for them, and re-layouts  1.35 us (2%)
  other arithmetic  1.33 us (2%)
    pallas_call x1, Pallas kernels, per_device(): pl.pallas_call(functools.partial(layer_kernel, names, dims), out_shape=ja...  67.7 us

profile of v1, /device:TPU:1, one launch (start us, length us, event | category | flops | bytes accessed | tf_op | source)
XLA Modules:
  0.0 70.4 jit_solution(4348543894530694656)
XLA Ops:
  0.0 1.3 %select_reduce_fusion = (s32[32]{0:T(128)}, s32[32]{0:T(128)}) fusion(s32[32]{0:T(128)} %param.18, s32[32]{0:T(128)} %param.17), kind=kLoop, calls=%fused_computation | loop fusion | flops 5056 | bytes 512 | tf_op jit(solution)/shard_map/reduce_sum | solution.py:444
  1.3 67.7 %latent_moe_layer.1 = bf16[28,288]{1,0:T(8,128)(2,1)} custom-call(s32[32]{0:T(128)} %get-tuple-element.6.refs_0_, s32[32]{0:T(128)} %get-tuple-element.5.refs_1_, bf16[144,192]{1,0:T(8,128)(2,1)} %bitcast.15, bf16[8,576,512]{2,1,0:T(8,128)(2,1)} %bitcast.12, bf16[32,24,576]{2,1,0:T(8,128)(2,1)} %refs_4_.1, bf16[16,128,512]{2,1,0:T(8,128)(2,1)} %refs_5_.1, ...), custom_call_target="tpu_custom_call" | custom-call | tf_op jit(solution)/shard_map/latent_moe_layer/pallas_call | solution.py:508
  69.1 1.3 %copy.16 = bf16[288,28]{0,1:T(8,128)(2,1)} copy(bf16[288,28]{0,1:T(8,128)(2,1)} %bitcast.14) | data formatting | bytes 32256

commit v2 on v1

v2 whole, which is shorter than its diff:
```python
import functools
import math
import types

import jax
import jax.numpy as jnp
from jax import lax
from jax.experimental import pallas as pl
from jax.experimental.pallas import tpu as pltpu
from jax.sharding import PartitionSpec as P

MESH = pl.DeviceIdType.MESH
F32 = jnp.float32
BF16 = jnp.bfloat16
RES = 8
SLOTS = 40
CORES = 2


def nn(a, b):
    return lax.dot_general(a, b, (((1,), (0,)), ((), ())), preferred_element_type=F32)


def nt(a, b):
    return lax.dot_general(a, b, (((1,), (1,)), ((), ())), preferred_element_type=F32)


def one_hot(mask):
    return jnp.where(mask, 1.0, 0.0).astype(BF16)


def iota(shape, dim):
    return lax.broadcasted_iota(jnp.int32, shape, dim)


def split2(value):
    high = value.astype(BF16).astype(F32)
    return high, (value - high).astype(BF16).astype(F32)


def layer_kernel(names, dims, *refs):
    (
        target_hbm, length_hbm, query_hbm, cache_hbm, moved_hbm, absorb_hbm, value_hbm, outproj_hbm,
        residual_hbm, gain_hbm, centroid_hbm, ids_hbm, up_hbm, down_hbm, out_ref,
    ) = refs[:15]
    s = types.SimpleNamespace(**dict(zip(names, refs[15:])))
    reps, heads, lines, xs, zs, groups, moved_n, columns, tokens, features = dims
    line_columns = columns * CORES * heads
    width = -(-line_columns // 128) * 128
    pitch = -(-columns // 16) * 16
    batch = tokens // reps
    half = lines * batch
    near = lines * RES
    kv = value_hbm.shape[1]
    nope = absorb_hbm.shape[1]
    qdim = query_hbm.shape[1]
    rope = qdim - nope
    full = kv + rope
    head_features = 16 * value_hbm.shape[2]
    scale = 1.0 / math.sqrt(qdim)

    rep = lax.axis_index("rep")
    head = lax.axis_index("head")
    line = rep // CORES
    core = rep % CORES
    lx = line // zs
    lz = line % zs
    owner = core * heads + head

    def rep_at(dx, dz, dc):
        return (((lx + dx) % xs) * zs + (lz + dz) % zs) * CORES + (core + dc) % CORES

    def line_at(dx, dz):
        return ((lx + dx) % xs) * zs + (lz + dz) % zs

    line_offsets = [(dx, dz) for dx in range(xs) for dz in range(zs) if (dx, dz) != (0, 0)]
    line_offsets.sort(key=lambda o: -(min(o[0], xs - o[0]) + min(o[1], zs - o[1])))
    plane_offsets = [(dx, dz, dc) for dx, dz in line_offsets for dc in range(CORES)]
    plane_offsets += [(0, 0, dc) for dc in range(1, CORES)]

    line_places = [(dc, dh) for dc in range(CORES) for dh in range(heads) if (dc, dh) != (0, 0)]

    def load(src, dst, sem):
        copy = pltpu.make_async_copy(src, dst, s.load_sem.at[sem])
        copy.start()
        return copy

    load_target = load(target_hbm, s.target, 0)
    load_length = load(length_hbm, s.length, 1)
    load_moved = load(moved_hbm, s.moved, 2)

    barrier = pltpu.get_barrier_semaphore()
    partners = [(rep_at(*o), head) for o in plane_offsets]
    for dh in range(1, heads):
        for dc in range(CORES):
            partners.append((rep_at(0, 0, dc), (head + dh) % heads))
    for partner in partners:
        pl.semaphore_signal(barrier, inc=1, device_id=partner, device_id_type=MESH)
    load_query = load(query_hbm, s.query, 3)
    load_absorb = load(absorb_hbm, s.absorb, 4)
    load_cache = load(cache_hbm, s.cache, 5)
    load_ids = load(ids_hbm, s.ids, 6)
    load_residual = load(residual_hbm, s.residual, 7)
    load_gain = load(gain_hbm, s.gain, 8)
    load_centroid = load(centroid_hbm, s.centroid, 9)
    load_outproj = load(outproj_hbm, s.outproj, 10)
    load_value = load(value_hbm, s.value, 11)

    load_target.wait()
    load_length.wait()
    matches = iota((groups, groups), 0) == s.target[...]
    source = jnp.sum(jnp.where(matches, iota((groups, groups), 1), 0), axis=1, keepdims=True)
    s.source_v[...] = jnp.broadcast_to(source, (groups, 128))
    load_source = load(s.source_v, s.source_s, 12)
    my_match = matches & (iota((groups, groups), 0) == rep)
    length = jnp.sum(jnp.sum(jnp.where(my_match, s.length[...], 0), axis=1, keepdims=True), axis=0, keepdims=True)
    load_source.wait()
    load_moved.wait()
    for g in range(groups):
        s.moved_out[g] = s.moved[jnp.clip(s.source_s[g, 0], 0, groups - 1)]


    pl.semaphore_wait(barrier, len(partners))

    def push(src, dst, phase, k, to_rep, to_head):
        copy = pltpu.make_async_remote_copy(
            src_ref=src, dst_ref=dst, send_sem=phase.at[0, k], recv_sem=phase.at[1, k],
            device_id=(to_rep, to_head), device_id_type=MESH,
        )
        copy.start()
        return copy

    rows_copies = []
    for k, offset in enumerate(plane_offsets):
        to_rep = rep_at(*offset)
        rows_copies.append(push(s.moved_out.at[to_rep], s.moved_in.at[rep], s.rows_sem, k, to_rep, head))

    load_query.wait()
    s.query_f[...] = s.query[:, pl.ds(0, nope)].astype(F32)
    s.joined[kv // 128, :, pl.ds(0, rope)] = s.query[:, pl.ds(nope, rope)].astype(F32)
    load_absorb.wait()
    for h in range(16):
        part = s.query_f[pl.ds(h, batch, stride=16), :].astype(BF16)
        absorbed = nn(part, s.absorb[h])
        for i in range(kv // 128):
            s.joined[i, pl.ds(h, batch, stride=16), :] = absorbed[:, 128 * i:128 * i + 128]

    def joined_query(i):
        parts = [s.joined[j, pl.ds(16 * i, 16), :] for j in range(kv // 128)]
        parts.append(s.joined[kv // 128, pl.ds(16 * i, 16), pl.ds(0, rope)])
        return jnp.concatenate(parts, axis=1).astype(BF16)

    def keep_latents(i, value):
        for j in range(kv // 128):
            s.latents[j, pl.ds(16 * i, 16), :] = value[:, 128 * j:128 * j + 128]

    s.far_query[...] = joined_query(RES)
    query_copies = []
    for dh in range(1, heads):
        query_copies.append(push(s.far_query, s.far_queries.at[head], s.query_sem, dh - 1, rep, (head + dh) % heads))
    s.far_queries[head] = s.far_query[...]

    load_outproj.wait()
    pad = jnp.zeros((pitch - columns, 512), F32)
    for i in range(outproj_hbm.shape[1] // 512):
        cut = s.outproj[:, pl.ds(512 * i, 512)].astype(F32)
        s.cols_out[:, pl.ds(512 * i, 512)] = jnp.concatenate([cut, pad], axis=0).astype(BF16)
    for copy in (load_residual, load_gain, load_centroid, load_ids):
        copy.wait()
    tok_lanes = -(-tokens // 128) * 128
    experts = centroid_hbm.shape[1]
    exp_lanes = -(-experts // 128) * 128
    s.static_out[...] = jnp.zeros_like(s.static_out)

    def padded(value):
        return jnp.concatenate([value.astype(F32), jnp.zeros((pitch - columns, value.shape[1]), F32)], axis=0).astype(BF16)

    s.static_out[:, pl.ds(0, tokens)] = padded(s.residual[...])
    s.static_out[:, pl.ds(tok_lanes, experts)] = padded(s.centroid[...])
    gain_row = jnp.broadcast_to(s.gain[...].astype(F32), (pitch, columns))
    diagonal = iota((pitch, columns), 0) == iota((pitch, columns), 1)
    gain_col = jnp.sum(jnp.where(diagonal, gain_row, 0.0), axis=1, keepdims=True)
    first_lane = iota((pitch, 128), 1) == 0
    s.static_out[:, pl.ds(tok_lanes + exp_lanes, 128)] = jnp.where(first_lane, gain_col, 0.0).astype(BF16)

    own_rows = pl.ds(pl.multiple_of(owner * pitch, pitch), pitch)
    cols_copies = []
    static_copies = []
    for dh in range(1, heads):
        to_head = (head + dh) % heads
        lanes = pl.ds(pl.multiple_of(to_head * head_features, 128), head_features)
        cols_copies.append(push(s.cols_out.at[:, lanes], s.cols_in.at[own_rows], s.cols_sem, dh - 1, rep, to_head))
        static_copies.append(push(s.static_out, s.static_in.at[own_rows], s.static_sem, dh - 1, rep, to_head))
    own_lanes = pl.ds(pl.multiple_of(head * head_features, 128), head_features)
    own_cols = pltpu.make_async_copy(s.cols_out.at[:, own_lanes], s.cols_in.at[own_rows], s.load_sem.at[13])
    own_cols.start()
    own_static = pltpu.make_async_copy(s.static_out, s.static_in.at[own_rows], s.load_sem.at[14])
    own_static.start()

    load_cache.wait()
    for i in range(RES):
        scores = nn(joined_query(i), s.cache[i]) * scale
        weights = jnp.exp(scores - jnp.max(scores, axis=1, keepdims=True))
        weights = (weights / jnp.sum(weights, axis=1, keepdims=True)).astype(BF16)
        keep_latents(i, nt(weights, s.cache[i, pl.ds(0, kv), :]))

    def head_outputs(start, count):
        for h in range(16):
            at = pl.ds(16 * start + h, count, stride=16) if count > 1 else pl.ds(16 * start + h, 1)
            parts = [s.latents[i, at, :] for i in range(kv // 128)]
            part = jnp.concatenate(parts, axis=1).astype(BF16)
            s.heads_f[at, :] = nn(part, s.value[h])
        return s.heads_f[pl.ds(16 * start, 16 * count), :].astype(BF16)

    load_value.wait()
    s.near_out[...] = head_outputs(0, RES)
    near_copies = []
    for k, (dx, dz) in enumerate(line_offsets):
        near_copies.append(push(s.near_out, s.near_in.at[line], s.near_sem, k, rep_at(dx, dz, 0), head))
    s.near_in[line] = s.near_out[...]
    load_up = load(up_hbm, s.up, 15)
    chunk = zs * line_columns
    load_down = [load(down_hbm.at[:, pl.ds(i * chunk, chunk)], s.down.at[i], 16 + i) for i in range(xs)]

    for copy in cols_copies + static_copies:
        copy.wait_recv()
    own_cols.wait()
    own_static.wait()
    core_rows = pl.ds(pl.multiple_of(core * (heads * pitch), heads * pitch), heads * pitch)
    other = rep_at(0, 0, 1)
    cols_pass = push(s.cols_in.at[core_rows], s.cols_in.at[core_rows], s.cols_sem, heads - 1, other, head)
    static_pass = push(s.static_in.at[core_rows], s.static_in.at[core_rows], s.static_sem, heads - 1, other, head)

    held = iota((tokens, tokens), 0)
    resident = held < CORES * near
    held_in = jnp.where(resident, held, held - CORES * near)
    held_size = jnp.where(resident, near, lines)
    held_core = jnp.where(held_in >= held_size, 1, 0)
    held_in = held_in - held_size * held_core
    held_line = jnp.where(resident, held_in >> 3, held_in)
    held_row = jnp.where(resident, held_in & (RES - 1), RES)
    order = batch * (CORES * held_line + held_core) + held_row
    reorder = one_hot(iota((tokens, tokens), 1) == order)
    s.reorder[...] = reorder
    named = jnp.zeros((lines, tokens), F32)
    my_experts = iota((lines, tokens), 0) * (CORES * heads) + owner
    for k in range(ids_hbm.shape[0]):
        named = jnp.where(my_experts == s.ids[pl.ds(k, 1), :], 1.0, named)
    earlier = one_hot(iota((tokens, tokens), 0) < iota((tokens, tokens), 1))
    slot = jnp.where(named > 0.0, nn(named.astype(BF16), earlier), -1.0)
    slot_index = iota((SLOTS, tokens), 0).astype(F32)
    pieces = [jnp.where(slot[e:e + 1, :] == slot_index, 1.0, 0.0) for e in range(lines)]
    s.gather[...] = jnp.concatenate(pieces, axis=0).astype(BF16)
    s.gather_held[...] = nt(s.gather[...], reorder).astype(BF16)
    eye = one_hot(iota((tokens, tokens), 0) == iota((tokens, tokens), 1))
    s.scatter[...] = nt(eye, s.gather[...]).astype(BF16)

    row_count = reps * moved_n
    pair = CORES * moved_n

    def keep_rows(from_line):
        both = [s.moved_in[from_line * CORES + c].astype(F32) for c in range(CORES)]
        s.rows_b[pl.ds(pl.multiple_of(from_line * pair, pair), pair), :] = jnp.concatenate(both, axis=0).astype(BF16)

    s.moved_in[rep] = s.moved_out[rep]
    rows_copies[-1].wait_recv()
    keep_rows(line)
    for i, (dx, dz) in enumerate(line_offsets):
        for copy in rows_copies[CORES * i:CORES * i + CORES]:
            copy.wait_recv()
        keep_rows(line_at(-dx, -dz))
    for copy in query_copies:
        copy.wait_recv()
    far_all = jnp.concatenate([s.far_queries[h] for h in range(heads)], axis=0)
    far_scores = nt(far_all, s.rows_b[...]) * scale
    place = iota((1, row_count), 1)
    from_device = (place * 2731) >> 16
    position = place + from_device * (moved_n * (heads - 1)) + head * moved_n
    far_scores = jnp.where(position < length, far_scores, -1e30)
    far_max = jnp.max(far_scores, axis=1, keepdims=True)
    far_weights = jnp.exp(far_scores - far_max)
    far_sum = jnp.sum(far_weights, axis=1, keepdims=True)
    s.far_out[:, pl.ds(0, kv)] = nn(far_weights.astype(BF16), s.rows_b[:, pl.ds(0, kv)]).astype(BF16)
    lane = iota((heads * 16, 128), 1)
    max_high = far_max.astype(BF16).astype(F32)
    max_mid = (far_max - max_high).astype(BF16).astype(F32)
    max_low = far_max - max_high - max_mid
    sum_high, sum_low = split2(far_sum)
    extras = jnp.zeros((heads * 16, 128), F32)
    for i, extra in enumerate((max_high, max_mid, max_low, sum_high, sum_low)):
        extras = jnp.where(lane == i, extra, extras)
    s.far_out[:, pl.ds(kv, 128)] = extras.astype(BF16)
    far_copies = []
    for dh in range(1, heads):
        to_head = (head + dh) % heads
        their_rows = pl.ds(pl.multiple_of(to_head * 16, 16), 16)
        far_copies.append(push(s.far_out.at[their_rows], s.far_in.at[head], s.far_sem, dh - 1, rep, to_head))
    s.far_in[head] = s.far_out[pl.ds(pl.multiple_of(head * 16, 16), 16), :]
    cols_pass.wait_recv()
    static_pass.wait_recv()
    row = iota((width, width), 0)
    col = iota((width, width), 1)
    squeeze = one_hot((row < line_columns) & (col == row + (pitch - columns) * ((row * 2341) >> 16)))
    for i in range(head_features // 512):
        cut = pl.ds(512 * i, 512)
        s.cols[:, cut] = nn(squeeze, s.cols_in[:, cut]).astype(BF16)
    static = nn(squeeze, s.static_in[...]).astype(BF16)
    s.residual_c[...] = nt(reorder, static[:, :tokens])
    their_expert = iota((lines, experts), 0) * (CORES * heads) + owner
    pick = one_hot(iota((lines, experts), 1) == their_expert)
    s.centroid_c[...] = nt(pick, static[:, tok_lanes:tok_lanes + experts])
    first = one_hot((iota((8, 128), 0) == 0) & (iota((8, 128), 1) == 0))
    s.gain_c[...] = nt(first, static[:, tok_lanes + exp_lanes:])
    for copy in far_copies:
        copy.wait_recv()
    extras = [s.far_in[h, :, pl.ds(kv, 128)].astype(F32) for h in range(heads)]
    maxima = [extra[:, 0:1] + extra[:, 1:2] + extra[:, 2:3] for extra in extras]
    top = functools.reduce(jnp.maximum, maxima)
    total = jnp.zeros((16, kv), F32)
    weight_sum = jnp.zeros((16, 1), F32)
    for h in range(heads):
        factor = jnp.exp(maxima[h] - top)
        total = total + factor * s.far_in[h, :, pl.ds(0, kv)].astype(F32)
        weight_sum = weight_sum + factor * (extras[h][:, 3:4] + extras[h][:, 4:5])
    keep_latents(RES, total / weight_sum)
    s.far_heads_out[...] = head_outputs(RES, 1)
    far_head_copies = []
    for k, (dx, dz) in enumerate(line_offsets):
        far_head_copies.append(push(s.far_heads_out, s.far_heads_in.at[line], s.heads_sem, k, rep_at(dx, dz, 0), head))
    s.far_heads_in[line] = s.far_heads_out[...]


    def project(copies, arrived, wide, count):
        for copy in copies:
            copy.wait_recv()
        wide[...] = arrived[...].astype(F32).reshape(wide.shape)
        acts = [wide[pl.ds(h, count, stride=16), :].astype(BF16) for h in range(16)]
        return nt(jnp.concatenate(acts, axis=1), s.cols[...])

    def spread_sum(part):
        s.sum_out[...] = part.astype(BF16)
        return [
            push(s.sum_out, s.sum_in.at[dh - 1], s.near_sum_sem, dh - 1, rep, (head + dh) % heads)
            for dh in range(1, heads)
        ]

    def swap_sum(part, copies):
        for dh, copy in enumerate(copies):
            copy.wait_recv()
            part = part + s.sum_in[dh].astype(F32)
        s.swap_out[...] = part
        return push(s.swap_out, s.swap_in, s.swap_sem, 0, other, head)

    near_part = project(near_copies, s.near_in, s.near_w, near)
    near_sums = spread_sum(near_part)
    far_part = project(far_head_copies, s.far_heads_in, s.far_w, lines)
    s.far_sum_out[...] = far_part.astype(BF16)
    far_sums = []
    for k, (dc, dh) in enumerate(line_places):
        far_sums.append(push(s.far_sum_out, s.far_sum_in.at[k], s.sum_sem, k, rep_at(0, 0, dc), (head + dh) % heads))
    near_swap = swap_sum(near_part, near_sums)
    first_core = core == 0
    near_tokens = CORES * near
    near_swap.wait_recv()

    def by_core(mine, theirs):
        return jnp.concatenate([jnp.where(first_core, mine, theirs), jnp.where(first_core, theirs, mine)], axis=0)

    def scaled_rows(attended, start, count):
        here = pl.ds(start, count)
        combined = s.residual_c[here, :] + attended
        s.combined[here, :] = combined
        square_high, square_low = split2(jnp.sum(combined * combined, axis=1, keepdims=True))
        scaled = combined * s.gain_c[0:1, :]
        token_lane = iota((count, width), 1)
        scaled = jnp.where(token_lane == line_columns, square_high, scaled)
        return jnp.where(token_lane == line_columns + 1, square_low, scaled).astype(BF16)

    near_scaled = scaled_rows(by_core(s.swap_out[...], s.swap_in[...]), 0, near_tokens)
    gathered = nn(s.gather_held[:, pl.ds(0, near_tokens)], near_scaled)
    far_mine = far_part
    far_theirs = jnp.zeros_like(far_part)
    for k, (dc, dh) in enumerate(line_places):
        far_sums[k].wait_recv()
        if dc == 0:
            far_mine = far_mine + s.far_sum_in[k].astype(F32)
        else:
            far_theirs = far_theirs + s.far_sum_in[k].astype(F32)
    far_scaled = scaled_rows(by_core(far_mine, far_theirs), near_tokens, CORES * lines)
    gathered = gathered + nn(s.gather_held[:, pl.ds(near_tokens, CORES * lines)], far_scaled)
    slot_lane = iota((SLOTS, width), 1)
    for e in range(lines):
        rows = gathered[SLOTS * e:SLOTS * e + SLOTS]
        high, low = split2(jnp.sum(rows * s.centroid_c[e:e + 1, :], axis=1, keepdims=True))
        rows = jnp.where(slot_lane == line_columns + 2, high, rows)
        rows = jnp.where(slot_lane == line_columns + 3, low, rows)
        s.tok_out[e] = rows.astype(BF16)
    tok_copies = []
    for k, (dx, dz) in enumerate(line_offsets):
        tok_copies.append(push(s.tok_out.at[line_at(dx, dz)], s.tok_in.at[line], s.tok_sem, k, rep_at(dx, dz, 0), head))
    s.tok_in[line] = s.tok_out[line]

    load_up.wait()
    inner = nn(s.tok_in[line][:, :line_columns], s.up[line])
    stats = s.tok_in[line].astype(F32)[:, width - 128:]
    for copy, (dx, dz) in zip(tok_copies, line_offsets):
        copy.wait_recv()
        from_line = line_at(-dx, -dz)
        rows = s.tok_in[from_line]
        inner = inner + nn(rows[:, :line_columns], s.up[from_line])
        stats = stats + rows.astype(F32)[:, width - 128:]
    at = line_columns - (width - 128)
    squares = stats[:, at:at + 1] + stats[:, at + 1:at + 2]
    logit = stats[:, at + 2:at + 3] + stats[:, at + 3:at + 4]
    root_mean = jnp.sqrt(squares / features + 1e-6)
    inner = inner / root_mean
    hidden = (inner * jax.nn.sigmoid(inner)).astype(BF16)
    affinity = jax.nn.sigmoid(logit / root_mean)
    affinity_high, affinity_low = split2(affinity)
    for copy in load_down:
        copy.wait()
    back_copies = []
    filler = jnp.zeros((SLOTS, width - line_columns), F32)
    x_order = sorted(range(xs), key=lambda dx: -min(dx, xs - dx))
    for dx in x_order:
        to_x = (lx + dx) % xs
        result = nn(hidden, s.down[to_x]) * affinity
        for z in range(zs):
            piece = jnp.concatenate([result[:, z * line_columns:(z + 1) * line_columns], filler], axis=1)
            piece = jnp.where(slot_lane == line_columns, affinity_high, piece)
            piece = jnp.where(slot_lane == line_columns + 1, affinity_low, piece)
            s.back_out[to_x * zs + z] = piece.astype(BF16)
        for dz in range(zs):
            if (dx, dz) != (0, 0):
                k = line_offsets.index((dx, dz))
                back_copies.append((k, push(s.back_out.at[line_at(dx, dz)], s.back_in.at[line], s.back_sem, k, rep_at(dx, dz, 0), head)))
    s.back_in[line] = s.back_out[line]
    rest = s.combined[...]
    my_columns = one_hot((iota((pitch, width), 0) < columns) & (iota((pitch, width), 1) == owner * columns + iota((pitch, width), 0)))
    combined_own = jnp.zeros((pitch, tokens), F32)
    for _ in range(3):
        part = rest.astype(BF16)
        rest = rest - part.astype(F32)
        combined_own = combined_own + nn(nt(my_columns, part).astype(BF16), s.reorder[...])
    s.combined_own[...] = combined_own

    for _, copy in back_copies:
        copy.wait_recv()

    returned = jnp.concatenate([s.back_in[e].astype(F32) for e in range(lines)], axis=0).astype(BF16)
    summed = nn(s.scatter[...], returned)
    token_lane = iota((tokens, width), 1)
    share_high, share_low = split2(summed[:, line_columns:line_columns + 1] + summed[:, line_columns + 1:line_columns + 2])
    summed = jnp.where(token_lane == line_columns, share_high, summed)
    summed = jnp.where(token_lane == line_columns + 1, share_low, summed)
    place_in = row & (pitch - 1)
    wanted = jnp.where(place_in < columns, row - (pitch - columns) * (row // pitch), line_columns + place_in - columns)
    spread = one_hot((col == wanted) & (place_in < columns + 2))
    pieces = nt(spread, summed.astype(BF16)).astype(BF16)
    for j in range(CORES * heads):
        s.last_out[j] = pieces[pitch * j:pitch * j + pitch]
    last_copies = []
    for k, (dc, dh) in enumerate(line_places):
        to_core, to_head = (core + dc) % CORES, (head + dh) % heads
        last_copies.append(push(
            s.last_out.at[to_core * heads + to_head], s.last_in.at[owner], s.last_sem, k, rep_at(0, 0, dc), to_head))
    s.last_in[owner] = s.last_out[owner]
    for copy in last_copies:
        copy.wait_recv()
    routed = s.last_in[0].astype(F32)
    for j in range(1, CORES * heads):
        routed = routed + s.last_in[j].astype(F32)
    share = routed[columns:columns + 1] + routed[columns + 1:columns + 2]
    layer_out = s.combined_own[...] + 2.5 * routed / share
    out_ref[...] = layer_out[:columns].astype(BF16)

    sends = rows_copies + cols_copies + static_copies + [cols_pass, static_pass] + query_copies + far_copies
    sends += near_copies + far_head_copies + near_sums + far_sums + [near_swap] + tok_copies + [copy for _, copy in back_copies] + last_copies
    for copy in sends:
        copy.wait_send()


def per_device(
    query, latent_cache, moved_rows, target_group, moved_length, key_absorb, value_head_projection,
    out_proj, residual, norm_gain, centroid, expert_ids, up_weight, down_weight,
):
    reps = lax.axis_size("rep")
    heads = lax.axis_size("head")
    lines = reps // CORES
    xs = 4 if lines % 4 == 0 else lines
    zs = lines // xs
    groups, moved_n, full = moved_rows.shape
    batch, local_heads, qdim = query.shape
    columns = out_proj.shape[1]
    tokens, topk = expert_ids.shape
    features, hidden = up_weight.shape[1:]
    experts = centroid.shape[0]
    kv = value_head_projection.shape[1]
    vd = value_head_projection.shape[2]
    context = latent_cache.shape[1]
    line_columns = columns * CORES * heads
    width = -(-line_columns // 128) * 128
    pitch = -(-columns // 16) * 16
    half = tokens // CORES
    tok_lanes = -(-tokens // 128) * 128
    static_lanes = tok_lanes + -(-experts // 128) * 128 + 128
    head_features = local_heads * vd

    vmem = dict(
        target=((1, groups), jnp.int32),
        length=((1, groups), jnp.int32),
        source_v=((groups, 128), jnp.int32),
        moved=((groups, moved_n, full), BF16),
        moved_out=((groups, moved_n, full), BF16),
        moved_in=((reps, moved_n, full), BF16),
        rows_b=((reps * moved_n, full), BF16),
        query=((batch * local_heads, qdim), BF16),
        query_f=((batch * local_heads, 128), F32),
        absorb=(key_absorb.shape, BF16),
        value=(value_head_projection.shape, BF16),
        cache=((latent_cache.shape[0], full, context), BF16),
        outproj=((columns, out_proj.shape[0]), BF16),
        cols_out=((pitch, out_proj.shape[0]), BF16),
        cols_in=((pitch * CORES * heads, head_features), BF16),
        cols=((width, head_features), BF16),
        residual=((columns, tokens), BF16),
        gain=((1, columns), BF16),
        centroid=((columns, experts), BF16),
        ids=((topk, tokens), jnp.int32),
        static_out=((pitch, static_lanes), BF16),
        static_in=((pitch * CORES * heads, static_lanes), BF16),
        residual_c=((tokens, width), F32),
        centroid_c=((lines, width), F32),
        gain_c=((8, width), F32),
        reorder=((tokens, tokens), BF16),
        gather=((lines * SLOTS, tokens), BF16),
        gather_held=((lines * SLOTS, tokens), BF16),
        scatter=((tokens, lines * SLOTS), BF16),
        joined=((kv // 128 + 1, batch * local_heads, 128), F32),
        latents=((kv // 128, batch * local_heads, 128), F32),
        heads_f=((batch * local_heads, vd), F32),
        near_out=((RES * local_heads, vd), BF16),
        near_in=((lines, RES * local_heads, vd), BF16),
        near_w=((lines * RES * local_heads, vd), F32),
        far_heads_out=((local_heads, vd), BF16),
        far_heads_in=((lines, local_heads, vd), BF16),
        far_w=((lines * local_heads, vd), F32),
        far_query=((local_heads, full), BF16),
        far_queries=((heads, local_heads, full), BF16),
        far_out=((heads * local_heads, kv + 128), BF16),
        far_in=((heads, local_heads, kv + 128), BF16),
        sum_out=((lines * RES, width), BF16),
        sum_in=((heads - 1, lines * RES, width), BF16),
        far_sum_out=((lines, width), BF16),
        far_sum_in=((CORES * heads - 1, lines, width), BF16),
        swap_out=((lines * RES, width), F32),
        swap_in=((lines * RES, width), F32),
        combined=((tokens, width), F32),
        combined_own=((pitch, tokens), F32),
        tok_out=((lines, SLOTS, width), BF16),
        tok_in=((lines, SLOTS, width), BF16),
        up=((lines, line_columns, hidden), BF16),
        down=((xs, hidden, zs * line_columns), BF16),
        back_out=((lines, SLOTS, width), BF16),
        back_in=((lines, SLOTS, width), BF16),
        last_out=((CORES * heads, pitch, tokens), BF16),
        last_in=((CORES * heads, pitch, tokens), BF16),
    )
    sems = dict(
        load_sem=(16 + xs,), rows_sem=(2, reps - 1), cols_sem=(2, heads), static_sem=(2, heads),
        query_sem=(2, heads - 1), far_sem=(2, heads - 1), heads_sem=(2, lines - 1), sum_sem=(2, CORES * heads - 1),
        swap_sem=(2, 1), near_sem=(2, lines - 1), near_sum_sem=(2, heads - 1), tok_sem=(2, lines - 1), back_sem=(2, lines - 1), last_sem=(2, CORES * heads - 1),
    )
    names = list(vmem) + ["source_s"] + list(sems)
    scratch = [pltpu.VMEM(shape, dtype) for shape, dtype in vmem.values()]
    scratch += [pltpu.SMEM((groups, 128), jnp.int32)]
    scratch += [pltpu.SemaphoreType.DMA(shape) for shape in sems.values()]
    dims = (reps, heads, lines, xs, zs, groups, moved_n, columns, tokens, features)
    layer_out = pl.pallas_call(
        functools.partial(layer_kernel, names, dims),
        out_shape=jax.ShapeDtypeStruct((columns, tokens), BF16),
        in_specs=[pl.BlockSpec(memory_space=pl.ANY)] * 14,
        out_specs=pl.BlockSpec(memory_space=pltpu.VMEM),
        scratch_shapes=scratch,
        compiler_params=pltpu.CompilerParams(
            collective_id=0, has_side_effects=True, vmem_limit_bytes=60 * 1024 * 1024
        ),
        name="latent_moe_layer",
    )(
        target_group.reshape(1, groups), moved_length.reshape(1, groups), query.reshape(batch * local_heads, qdim), jnp.swapaxes(latent_cache, 1, 2), moved_rows,
        key_absorb, value_head_projection, out_proj.T, residual.T, norm_gain.reshape(1, columns), centroid.T,
        expert_ids.T, up_weight.reshape(lines, line_columns, hidden), down_weight[0],
    )
    return layer_out.T


def solution(mesh):
    return jax.shard_map(
        per_device,
        mesh=mesh,
        in_specs=(
            P("rep", "head", None),
            P("rep", None, None),
            P(None, ("rep", "head"), None),
            P(),
            P(),
            P("head", None, None),
            P("head", None, None),
            P(None, ("rep", "head")),
            P(None, ("rep", "head")),
            P(("rep", "head")),
            P(None, ("rep", "head")),
            P(),
            P(("rep", "head"), None, None),
            P(("rep", "head"), None, None),
        ),
        out_specs=P(None, ("rep", "head")),
        check_vma=False,
    )
```

time: 70.6 us -> 62.1 us (0.88)
  Pallas kernels: 67.7 us -> 60.6 us
  other arithmetic: 1.33 us -> 0 us
    pallas_call x1, Pallas kernels: 67.7 us -> 60.6 us  [per_device(): pl.pallas_call(functools.partial(layer_kernel, names, dims), out_shape=ja...]
    reduce_sum x1 -> x0, other arithmetic: 1.33 us -> none  [per_device(): length = jnp.sum(jnp.where(match, moved_length[None, :], 0), axis=1)]
where the time goes in v2:
time: 62.1 us; the launch traced here: 61.9 us
  Pallas kernels  60.6 us (98%)
  local copies, waits for them, and re-layouts  1.35 us (2%)
    pallas_call x1, Pallas kernels, per_device(): pl.pallas_call(functools.partial(layer_kernel, names, dims), out_shape=ja...  60.6 us
    unnamed x1, local copies, waits for them, and re-layouts  1.35 us

profile of v2, /device:TPU:1, one launch (start us, length us, event | category | flops | bytes accessed | tf_op | source)
XLA Modules:
  0.0 61.9 jit_solution(5714314623162887397)
XLA Ops:
  0.0 60.6 %latent_moe_layer.1 = bf16[28,288]{1,0:T(8,128)(2,1)} custom-call(s32[1,32]{1,0:T(1,128)} %bitcast.21, s32[1,32]{1,0:T(1,128)} %bitcast.22, bf16[144,192]{1,0:T(8,128)(2,1)} %bitcast.17, bf16[8,576,512]{2,1,0:T(8,128)(2,1)} %bitcast.14, bf16[32,24,576]{2,1,0:T(8,128)(2,1)} %refs_4_.1, bf16[16,128,512]{2,1,0:T(8,128)(2,1)} %refs_5_.1, ...), custom_call_target="tpu_custom_call" | custom-call | tf_op jit(solution)/shard_map/latent_moe_layer/pallas_call | solution.py:579
  60.6 1.3 %copy.16 = bf16[288,28]{0,1:T(8,128)(2,1)} copy(bf16[288,28]{0,1:T(8,128)(2,1)} %bitcast.16) | data formatting | bytes 32256

commit v3 on v2

--- a/solution.py
+++ b/solution.py
@@ -67,11 +67,15 @@
     lz = line % zs
     owner = core * heads + head
 
+    next_x = [(lx + d) % xs for d in range(xs)]
+    next_z = [(lz + d) % zs for d in range(zs)]
+    next_core = [(core + d) % CORES for d in range(CORES)]
+
+    def line_at(dx, dz):
+        return next_x[dx % xs] * zs + next_z[dz % zs]
+
     def rep_at(dx, dz, dc):
-        return (((lx + dx) % xs) * zs + (lz + dz) % zs) * CORES + (core + dc) % CORES
-
-    def line_at(dx, dz):
-        return ((lx + dx) % xs) * zs + (lz + dz) % zs
+        return line_at(dx, dz) * CORES + next_core[dc % CORES]
 
     line_offsets = [(dx, dz) for dx in range(xs) for dz in range(zs) if (dx, dz) != (0, 0)]
     line_offsets.sort(key=lambda o: -(min(o[0], xs - o[0]) + min(o[1], zs - o[1])))
@@ -94,7 +98,17 @@
     for dh in range(1, heads):
         for dc in range(CORES):
             partners.append((rep_at(0, 0, dc), (head + dh) % heads))
-    for partner in partners:
+    for partner in partners[:12]:
+        pl.semaphore_signal(barrier, inc=1, device_id=partner, device_id_type=MESH)
+    load_target.wait()
+    load_length.wait()
+    matches = iota((groups, groups), 0) == s.target[...]
+    source = jnp.sum(jnp.where(matches, iota((groups, groups), 1), 0), axis=1, keepdims=True)
+    s.source_v[...] = jnp.broadcast_to(source, (groups, 128))
+    load_source = load(s.source_v, s.source_s, 12)
+    my_match = matches & (iota((groups, groups), 0) == rep)
+    length = jnp.sum(jnp.sum(jnp.where(my_match, s.length[...], 0), axis=1, keepdims=True), axis=0, keepdims=True)
+    for partner in partners[12:]:
         pl.semaphore_signal(barrier, inc=1, device_id=partner, device_id_type=MESH)
     load_query = load(query_hbm, s.query, 3)
     load_absorb = load(absorb_hbm, s.absorb, 4)
@@ -106,14 +120,6 @@
     load_outproj = load(outproj_hbm, s.outproj, 10)
     load_value = load(value_hbm, s.value, 11)
 
-    load_target.wait()
-    load_length.wait()
-    matches = iota((groups, groups), 0) == s.target[...]
-    source = jnp.sum(jnp.where(matches, iota((groups, groups), 1), 0), axis=1, keepdims=True)
-    s.source_v[...] = jnp.broadcast_to(source, (groups, 128))
-    load_source = load(s.source_v, s.source_s, 12)
-    my_match = matches & (iota((groups, groups), 0) == rep)
-    length = jnp.sum(jnp.sum(jnp.where(my_match, s.length[...], 0), axis=1, keepdims=True), axis=0, keepdims=True)
     load_source.wait()
     load_moved.wait()
     for g in range(groups):
@@ -389,16 +395,25 @@
     far_scaled = scaled_rows(by_core(far_mine, far_theirs), near_tokens, CORES * lines)
     gathered = gathered + nn(s.gather_held[:, pl.ds(near_tokens, CORES * lines)], far_scaled)
     slot_lane = iota((SLOTS, width), 1)
-    for e in range(lines):
-        rows = gathered[SLOTS * e:SLOTS * e + SLOTS]
-        high, low = split2(jnp.sum(rows * s.centroid_c[e:e + 1, :], axis=1, keepdims=True))
+    s.gathered[...] = gathered
+
+    def fill_rows(to_line):
+        rows = s.gathered[pl.ds(pl.multiple_of(to_line * SLOTS, SLOTS), SLOTS), :]
+        high, low = split2(jnp.sum(rows * s.centroid_c[pl.ds(to_line, 1), :], axis=1, keepdims=True))
         rows = jnp.where(slot_lane == line_columns + 2, high, rows)
         rows = jnp.where(slot_lane == line_columns + 3, low, rows)
-        s.tok_out[e] = rows.astype(BF16)
+        return rows.astype(BF16)
+
     tok_copies = []
     for k, (dx, dz) in enumerate(line_offsets):
-        tok_copies.append(push(s.tok_out.at[line_at(dx, dz)], s.tok_in.at[line], s.tok_sem, k, rep_at(dx, dz, 0), head))
-    s.tok_in[line] = s.tok_out[line]
+        to_line = line_at(dx, dz)
+        s.tok_out[to_line] = fill_rows(to_line)
+        tok_copies.append(push(s.tok_out.at[to_line], s.tok_in.at[line], s.tok_sem, k, rep_at(dx, dz, 0), head))
+    s.tok_in[line] = fill_rows(line)
+    sent = rows_copies + cols_copies + static_copies + [cols_pass, static_pass] + query_copies + far_copies
+    sent += near_copies + far_head_copies + near_sums + far_sums + [near_swap]
+    for copy in sent:
+        copy.wait_send()
 
     load_up.wait()
     inner = nn(s.tok_in[line][:, :line_columns], s.up[line])
@@ -420,6 +435,15 @@
     for copy in load_down:
         copy.wait()
     back_copies = []
+
+    def steps_to(offset):
+        return min(offset[0], xs - offset[0]) + min(offset[1], zs - offset[1])
+
+    def send_back(places):
+        for k in places:
+            dx, dz = line_offsets[k]
+            back_copies.append(push(s.back_out.at[line_at(dx, dz)], s.back_in.at[line], s.back_sem, k, rep_at(dx, dz, 0), head))
+
     filler = jnp.zeros((SLOTS, width - line_columns), F32)
     x_order = sorted(range(xs), key=lambda dx: -min(dx, xs - dx))
     for dx in x_order:
@@ -430,10 +454,8 @@
             piece = jnp.where(slot_lane == line_columns, affinity_high, piece)
             piece = jnp.where(slot_lane == line_columns + 1, affinity_low, piece)
             s.back_out[to_x * zs + z] = piece.astype(BF16)
-        for dz in range(zs):
-            if (dx, dz) != (0, 0):
-                k = line_offsets.index((dx, dz))
-                back_copies.append((k, push(s.back_out.at[line_at(dx, dz)], s.back_in.at[line], s.back_sem, k, rep_at(dx, dz, 0), head)))
+        send_back([k for k, offset in enumerate(line_offsets) if offset[0] == dx and steps_to(offset) > 2])
+    send_back([k for k, offset in enumerate(line_offsets) if steps_to(offset) <= 2])
     s.back_in[line] = s.back_out[line]
     rest = s.combined[...]
     my_columns = one_hot((iota((pitch, width), 0) < columns) & (iota((pitch, width), 1) == owner * columns + iota((pitch, width), 0)))
@@ -444,7 +466,9 @@
         combined_own = combined_own + nn(nt(my_columns, part).astype(BF16), s.reorder[...])
     s.combined_own[...] = combined_own
 
-    for _, copy in back_copies:
+    for copy in tok_copies:
+        copy.wait_send()
+    for copy in back_copies:
         copy.wait_recv()
 
     returned = jnp.concatenate([s.back_in[e].astype(F32) for e in range(lines)], axis=0).astype(BF16)
@@ -465,6 +489,8 @@
         last_copies.append(push(
             s.last_out.at[to_core * heads + to_head], s.last_in.at[owner], s.last_sem, k, rep_at(0, 0, dc), to_head))
     s.last_in[owner] = s.last_out[owner]
+    for copy in back_copies:
+        copy.wait_send()
     for copy in last_copies:
         copy.wait_recv()
     routed = s.last_in[0].astype(F32)
@@ -474,9 +500,7 @@
     layer_out = s.combined_own[...] + 2.5 * routed / share
     out_ref[...] = layer_out[:columns].astype(BF16)
 
-    sends = rows_copies + cols_copies + static_copies + [cols_pass, static_pass] + query_copies + far_copies
-    sends += near_copies + far_head_copies + near_sums + far_sums + [near_swap] + tok_copies + [copy for _, copy in back_copies] + last_copies
-    for copy in sends:
+    for copy in last_copies:
         copy.wait_send()
 
 
@@ -557,6 +581,7 @@
         swap_in=((lines * RES, width), F32),
         combined=((tokens, width), F32),
         combined_own=((pitch, tokens), F32),
+        gathered=((lines * SLOTS, width), F32),
         tok_out=((lines, SLOTS, width), BF16),
         tok_in=((lines, SLOTS, width), BF16),
         up=((lines, line_columns, hidden), BF16),

time: 62.1 us -> 62.2 us (level)
  no operation moved by 1% of the time
where the time goes in v3:
time: 62.2 us; the launch traced here: 62 us
  Pallas kernels  60.6 us (97%)
  local copies, waits for them, and re-layouts  1.35 us (2%)
    pallas_call x1, Pallas kernels, per_device(): pl.pallas_call(functools.partial(layer_kernel, names, dims), out_shape=ja...  60.6 us
    unnamed x1, local copies, waits for them, and re-layouts  1.35 us

profile of v3, /device:TPU:1, one launch (start us, length us, event | category | flops | bytes accessed | tf_op | source)
XLA Modules:
  0.0 62.0 jit_solution(16603025764234729415)
XLA Ops:
  0.0 60.6 %latent_moe_layer.1 = bf16[28,288]{1,0:T(8,128)(2,1)} custom-call(s32[1,32]{1,0:T(1,128)} %bitcast.21, s32[1,32]{1,0:T(1,128)} %bitcast.22, bf16[144,192]{1,0:T(8,128)(2,1)} %bitcast.17, bf16[8,576,512]{2,1,0:T(8,128)(2,1)} %bitcast.14, bf16[32,24,576]{2,1,0:T(8,128)(2,1)} %refs_4_.1, bf16[16,128,512]{2,1,0:T(8,128)(2,1)} %refs_5_.1, ...), custom_call_target="tpu_custom_call" | custom-call | tf_op jit(solution)/shard_map/latent_moe_layer/pallas_call | solution.py:604
  60.6 1.3 %copy.16 = bf16[288,28]{0,1:T(8,128)(2,1)} copy(bf16[288,28]{0,1:T(8,128)(2,1)} %bitcast.16) | data formatting | bytes 32256
